TPU v7x, 256 devices: a whole 4x4x8 slice. The times are simulated.
256 devices in a mesh: blk: 128 (over y, x_hi, z, core), rhs: 2 (over x_lo).
Axes of the slice: x: 4 (x_hi: 2, x_lo: 2; x = x_hi * 2 + x_lo), y: 4, z: 8, core: 2. Of those that a mesh axis runs over, the one named last changes fastest.
Arguments:
- directions: bfloat16 [262144, 256], P('blk', 'rhs'), may hold values from -6 to 6
- axial_pos: bfloat16 [262144], P('blk'), may hold values from 0 to 8
- azimuth: bfloat16 [262144], P('blk'), may hold values from -3.140625 to 3.140625
- panel_area: bfloat16 [262144], P('blk'), may hold values from 0.5 to 2
Outputs:
- product: float32 [262144, 256], P('blk', 'rhs')
- gram: float32 [256, 256], P(None, 'rhs')
All inputs are finite; a program needn't handle non-finite values.
Results may differ from a plain program's by a relative error of at most 0.0029.
Values may be sent and summed in bfloat16 or wider, within the bound.
No kernel may reach another device: no remote copies, remote signals or barrier semaphores. Data moves between devices by JAX's collectives and lax.ppermute only.
A program may use at most 64 MiB of HBM per device.

v0:
```python
import math

import jax
import jax.numpy as jnp
from jax import lax
from jax.sharding import PartitionSpec as P

ROUNDS = 3


def shifted(value, axis, steps):
    count = lax.axis_size(axis)
    pairs = [(source, (source + steps) % count) for source in range(count)]
    return lax.ppermute(value, axis, pairs)


def kernel_tile(row_geom, col_geom, count):
    row_axial, row_cos, row_sin, row_weight = row_geom
    col_axial, col_cos, col_sin, col_weight = col_geom
    delta_a = row_axial[:, None] - col_axial[None, :]
    delta_c = row_cos[:, None] - col_cos[None, :]
    delta_s = row_sin[:, None] - col_sin[None, :]
    square = delta_a * delta_a + delta_c * delta_c + delta_s * delta_s
    weights = row_weight[:, None] * col_weight[None, :]
    value = weights * lax.rsqrt(square + 0.01) / jnp.sqrt(jnp.float32(count))
    return value.astype(jnp.bfloat16)


def panel_points(axial_pos, azimuth, panel_area):
    angle_f = azimuth.astype(jnp.float32)
    return (
        axial_pos.astype(jnp.float32),
        jnp.cos(angle_f),
        jnp.sin(angle_f),
        panel_area.astype(jnp.float32),
    )


def apply_tile(home_geom, other_geom, other_dirs, home_dirs, with_back, count):
    row_total = home_dirs.shape[0]
    width = home_dirs.shape[1]
    row_step = math.gcd(row_total, 512)
    blocks = row_total // row_step
    split_geom = tuple((part.reshape(blocks, row_step) for part in home_geom))
    split_dirs = home_dirs.reshape(blocks, row_step, width)

    def step_fn(carried, item):
        row_axial, row_cos, row_sin, row_weight, row_dirs = item
        values = kernel_tile((row_axial, row_cos, row_sin, row_weight), other_geom, count)
        forward = jnp.dot(values, other_dirs, preferred_element_type=jnp.float32)
        if with_back:
            carried = carried + lax.dot_general(
                values, row_dirs, (((0,), (0,)), ((), ())), preferred_element_type=jnp.float32
            )
        return (carried, forward)

    start = jnp.zeros((other_dirs.shape[0], width), jnp.float32)
    backward, pieces = lax.scan(step_fn, start, split_geom + (split_dirs,))
    return (pieces.reshape(row_total, other_dirs.shape[1]), backward)


def shards(directions, axial_pos, azimuth, panel_area):
    count = axial_pos.shape[0]
    home_geom = panel_points(axial_pos, azimuth, panel_area)
    whole = lax.all_gather(directions, "rhs", axis=1, tiled=True)
    product, unused_back = apply_tile(home_geom, home_geom, directions, directions, False, count)
    for shift_by in range(1, ROUNDS + 1):
        guest_dirs, guest_axial, guest_angle, guest_area = shifted(
            (directions, axial_pos, azimuth, panel_area), "blk", shift_by
        )
        forward, backward = apply_tile(
            home_geom,
            panel_points(guest_axial, guest_angle, guest_area),
            guest_dirs,
            directions,
            True,
            count,
        )
        product = product + forward
        product = product + shifted(backward, "blk", -shift_by)
    partial_value = jnp.dot(whole.astype(jnp.float32).T, product, precision=lax.Precision.HIGHEST)
    gram = lax.psum(partial_value, "blk") / (count * lax.axis_size("blk"))
    return (product, gram)


def solution(mesh):
    in_specs = (P("blk", "rhs"), P("blk"), P("blk"), P("blk"))
    out_specs = (P("blk", "rhs"), P(None, "rhs"))
    return jax.shard_map(shards, mesh=mesh, in_specs=in_specs, out_specs=out_specs, check_vma=False)
```

profile of v0, /device:TPU:1, one launch (start us, length us, event | category | flops | bytes accessed | tf_op | source)
XLA Modules:
  0.0 1295.6 jit_solution(15935273825989977719)
XLA Ops:
  21.9 3.8 collective-permute-start.12
  29.7 5.9 collective-permute-done.10
  35.9 25.9 %while.50 = (s32[]{:T(128)}, f32[2048,128]{1,0:T(8,128)}, f32[4,512,128]{2,1,0:T(8,128)S(1)}, f32[4,512]{1,0:T(4,128)S(1)}, f32[2048]{0:T(1024)S(1)}, /*index=5*...) while((s32[]{:T(128)}, f32[2048,128]{1,0:T(8,128)}, ...), condition=%wide.region_3.4_spmd.clone, body=%wide.region_2.3_spmd.clone.sunk | while | flops 564658176 | bytes 3113635 | solution.py:58
  38.0 4.1 convolution_add_fusion.6
  44.2 4.5 convolution_add_fusion.6
  50.7 4.5 convolution_add_fusion.6
  57.3 4.5 convolution_add_fusion.6
  61.8 4.3 collective-permute-start.4
  67.0 30.0 %while.51 = (s32[]{:T(128)}, f32[2048,128]{1,0:T(8,128)}, f32[4,512,128]{2,1,0:T(8,128)S(1)}, f32[4,512]{1,0:T(4,128)S(1)}, f32[2048]{0:T(1024)S(1)}, /*index=5*...) while((s32[]{:T(128)}, f32[2048,128]{1,0:T(8,128)}, ...), condition=%wide.region_5.6_spmd.clone, body=%wide.region_4.5_spmd.clone.sunk | while | flops 564658176 | bytes 3113635 | solution.py:58
  70.1 4.1 convolution_add_fusion.7
  77.3 4.5 convolution_add_fusion.7
  84.9 4.5 convolution_add_fusion.7
  92.5 4.5 convolution_add_fusion.7
  101.3 30.0 %while.52 = (s32[]{:T(128)}, f32[2048,128]{1,0:T(8,128)}, f32[4,512,128]{2,1,0:T(8,128)S(1)}, f32[4,512]{1,0:T(4,128)S(1)}, f32[2048]{0:T(1024)S(1)}, /*index=5*...) while((s32[]{:T(128)}, f32[2048,128]{1,0:T(8,128)}, ...), condition=%wide.region_7.8_spmd.clone, body=%wide.region_6.7_spmd.clone.sunk | while | flops 564658176 | bytes 3113635 | solution.py:58
  104.5 4.1 convolution_add_fusion.8
  111.7 4.5 convolution_add_fusion.8
  119.2 4.5 convolution_add_fusion.8
  126.8 4.5 convolution_add_fusion.8
  135.4 15.3 %while.49 = (s32[]{:T(128)}, f32[4,512,128]{2,1,0:T(8,128)}, f32[4,512]{1,0:T(4,128)S(1)}, f32[2048]{0:T(1024)S(1)}, f32[4,512]{1,0:T(4,128)S(1)}, /*index=5*/f3...) while((s32[]{:T(128)}, f32[4,512,128]{2,1,0:T(8,128)}, ...), condition=%wide.region_1.2_spmd, body=%wide.region_0.1_spmd.sunk | while | flops 282066944 | bytes 844413 | solution.py:58
  135.4 3.8 fusion.49
  139.2 3.8 fusion.49
  143.1 3.8 fusion.49
  152.0 16.4 %collective-permute-done.14 = f32[2048,128]{1,0:T(8,128)} collective-permute-done((f32[2048,128]{1,0:T(8,128)}, f32[2048,128]{1,0:T(8,128)}, u32[]{:S(2)}, u32[]{:S(2)}) %collective-permute-start.14) | collective-permute-done | bytes 1048608 | tf_op jit(solution)/shard_map/ppermute | solution.py:14
  174.0 1113.1 %all-reduce.2.cloned.1.call-done = f32[256,128]{0,1:T(8,128)} async-done(((f32[256,128]{0,1:T(8,128)}), f32[256,128]{0,1:T(8,128)}) %all-reduce.2.cloned.1.call-update) | async-done | bytes 131088 | tf_op jit(solution)/shard_map/psum | solution.py:82
  (110 shorter events, 73.4 us)
Async XLA Ops:
  7.2 163.6 %all-gather.2.cloned.1.call-start = ((), (), s32[]{:S(2)}) async-start(), calls=%async_computation | async-start | bytes 1572864 | tf_op jit(solution)/shard_map/all_gather | solution.py:65
  7.2 10.8 collective-permute-start.2
  10.3 15.4 %collective-permute-start.7 = (bf16[2048]{0:T(1024)(128)(2,1)}, bf16[2048]{0:T(1024)(128)(2,1)S(1)}, u32[]{:S(2)}, u32[]{:S(2)}) collective-permute-start(bf16[2048]{0:T(1024)(128)(2,1)} %param.14), channel_id=1, source_target_pairs={{0,4},{2,6},{4,8},{6,10},{8,12},{10,14},{12,16},{14,18},{16,20},{1... | collective-permute-start | bytes 12296 | tf_op jit(solution)/shard_map/ppermute | solution.py:14
  12.0 23.9 %collective-permute-start.3 = (bf16[2048,128]{1,0:T(8,128)(2,1)}, bf16[2048,128]{1,0:T(8,128)(2,1)S(1)}, u32[]{:S(2)}, u32[]{:S(2)}) collective-permute-start(bf16[2048,128]{1,0:T(8,128)(2,1)} %param.12), channel_id=1, source_target_pairs={{0,2},{2,4},{4,6},{6,8},{8,10},{10,12},{12,14},{14,16},{16,18},{18... | collective-permute-start | bytes 1572872 | tf_op jit(solution)/shard_map/ppermute | solution.py:14
  12.3 1274.8 %all-reduce.2.cloned.1.call-start = ((), (), s32[]{:S(2)}) async-start(), calls=%async_computation.1 | async-start | bytes 262144 | tf_op jit(solution)/shard_map/psum | solution.py:82
  12.4 8.6 collective-permute-start
  14.1 7.7 collective-permute-start.1
  18.0 8.5 collective-permute-start.5
  21.0 8.6 collective-permute-start.6
  21.9 13.9 %collective-permute-start.12 = (bf16[2048]{0:T(1024)(128)(2,1)}, bf16[2048]{0:T(1024)(128)(2,1)S(1)}, u32[]{:S(2)}, u32[]{:S(2)}) collective-permute-start(bf16[2048]{0:T(1024)(128)(2,1)} %param.14), channel_id=1, source_target_pairs={{0,6},{2,8},{4,10},{6,12},{8,14},{10,16},{12,18},{14,20},{16,22},{... | collective-permute-start | bytes 12296 | tf_op jit(solution)/shard_map/ppermute | solution.py:14
  25.7 9.9 collective-permute-start.10
  26.5 9.3 collective-permute-start.11
  29.6 36.4 %collective-permute-start.8 = (bf16[2048,128]{1,0:T(8,128)(2,1)}, bf16[2048,128]{1,0:T(8,128)(2,1)S(1)}, u32[]{:S(2)}, u32[]{:S(2)}) collective-permute-start(bf16[2048,128]{1,0:T(8,128)(2,1)} %param.12), channel_id=1, source_target_pairs={{0,4},{2,6},{4,8},{6,10},{8,12},{10,14},{12,16},{14,18},{16,20},{1... | collective-permute-start | bytes 1572872 | tf_op jit(solution)/shard_map/ppermute | solution.py:14
  35.6 64.9 %collective-permute-start.13 = (bf16[2048,128]{1,0:T(8,128)(2,1)}, bf16[2048,128]{1,0:T(8,128)(2,1)S(1)}, u32[]{:S(2)}, u32[]{:S(2)}) collective-permute-start(bf16[2048,128]{1,0:T(8,128)(2,1)} %param.12), channel_id=1, source_target_pairs={{0,6},{2,8},{4,10},{6,12},{8,14},{10,16},{12,18},{14,20},{16,22},{... | collective-permute-start | bytes 1572872 | tf_op jit(solution)/shard_map/ppermute | solution.py:14
  61.8 90.2 %collective-permute-start.4 = (f32[2048,128]{1,0:T(8,128)}, f32[2048,128]{1,0:T(8,128)}, u32[]{:S(2)}, u32[]{:S(2)}) collective-permute-start(f32[2048,128]{1,0:T(8,128)} %get-tuple-element.265), channel_id=1, source_target_pairs={{0,254},{2,0},{4,2},{6,4},{8,6},{10,8},{12,10},{14,12},{16,14},{18... | collective-permute-start | bytes 3145736 | tf_op jit(solution)/shard_map/ppermute | solution.py:14
  66.1 0.8 copy-start.2
  97.0 55.0 %collective-permute-start.9 = (f32[2048,128]{1,0:T(8,128)}, f32[2048,128]{1,0:T(8,128)}, u32[]{:S(2)}, u32[]{:S(2)}) collective-permute-start(f32[2048,128]{1,0:T(8,128)} %get-tuple-element.267), channel_id=1, source_target_pairs={{0,252},{2,254},{4,0},{6,2},{8,4},{10,6},{12,8},{14,10},{16,12},{1... | collective-permute-start | bytes 3145736 | tf_op jit(solution)/shard_map/ppermute | solution.py:14
  100.5 0.8 copy-start.1
  131.3 37.1 %collective-permute-start.14 = (f32[2048,128]{1,0:T(8,128)}, f32[2048,128]{1,0:T(8,128)}, u32[]{:S(2)}, u32[]{:S(2)}) collective-permute-start(f32[2048,128]{1,0:T(8,128)} %get-tuple-element.269), channel_id=1, source_target_pairs={{0,250},{2,252},{4,254},{6,0},{8,2},{10,4},{12,6},{14,8},{16,10},{... | collective-permute-start | bytes 3145736 | tf_op jit(solution)/shard_map/ppermute | solution.py:14
  170.7 3.3 copy-start
Sparse Core Ops, SparseCore 0:
  12.5 44.6 all-gather.1
  174.1 1112.9 all-reduce.1
where the time goes:
time: 1300 us
  waiting for transfers between devices  1140 us (88%)
  matrix products  104 us (8%)
  starting transfers between devices  27.1 us (2%)
  between operations  14.2 us (1%)
    psum x1, waiting for transfers between devices, shards(): gram = lax.psum(partial_value, 'blk') / (count * lax.axis_size('blk'))  1110 us
    dot_general x12, matrix products, step_fn(): lax.dot_general(values, row_dirs, (((0,), (0,)), ((), ())), preferred_ele...  52.7 us
    dot_general x16, matrix products, step_fn(): forward = jnp.dot(values, other_dirs, preferred_element_type=jnp.float32)  47.7 us
    ppermute x15, starting transfers between devices, shifted(): return lax.ppermute(value, axis, pairs)  27.1 us
  transfers between devices with their start and end apart: 17, of which 6 were waited for; matrix products, arithmetic and copies ran while one was open for 8% of the time, Pallas kernels for 0%

commit v1 on v0

v1 whole, which is shorter than its diff:
```python
import functools

import jax
import jax.numpy as jnp
from jax import lax
from jax.experimental import pallas as pl
from jax.experimental.pallas import tpu as pltpu
from jax.sharding import Mesh, PartitionSpec as P

LANES = 128
VMEM_BYTES = 24 * 2**20
ROW_STEP = 1024
COL_STEP = 256
BLK = ("y", "xh", "z", "core")


def split_parts(base):
    high = base.astype(jnp.bfloat16).astype(jnp.float32)
    rest = base - high
    mid = rest.astype(jnp.bfloat16).astype(jnp.float32)
    low = (rest - mid).astype(jnp.bfloat16).astype(jnp.float32)
    return high, mid, low


def point_values(axial, angle, area):
    axial = axial.astype(jnp.float32) - 4.0
    angle = angle.astype(jnp.float32)
    area = area.astype(jnp.float32)
    cos, sin = jnp.cos(angle), jnp.sin(angle)
    return axial, cos, sin, axial * axial + cos * cos + sin * sin, 1.0 / (area * area)


def lay_rows(base_ref, features):
    groups = features[0].shape[0]
    base_ref[...] = jnp.zeros_like(base_ref)
    for row, feature in enumerate(features):
        for group in range(groups):
            base_ref[row : row + 1, group * LANES : (group + 1) * LANES] = feature[group : group + 1, :]


def column_factors(geometry, base_ref, col_ref):
    axial, cos, sin, norm, scale = point_values(*geometry)
    lay_rows(base_ref, (scale, norm * scale, axial * scale, cos * scale, sin * scale))
    high, mid, low = split_parts(base_ref[...])
    col_ref[...] = jnp.concatenate([high, high, high, mid, mid, low], axis=0).astype(jnp.bfloat16)


def row_factors(geometry, base_ref, row_ref):
    axial, cos, sin, norm, scale = point_values(*geometry)
    count = base_ref.shape[1]
    scale = scale * count
    double = -2.0 * scale
    lay_rows(base_ref, ((norm + 0.01) * scale, scale, axial * double, cos * double, sin * double))
    high, mid, low = split_parts(base_ref[...])
    stacked = jnp.concatenate([high, mid, low, high, mid, high], axis=0)
    for group in range(count // LANES):
        part = stacked[:, group * LANES : (group + 1) * LANES]
        row_ref[group * LANES : (group + 1) * LANES, :] = part.T.astype(jnp.bfloat16)


def tile_product(row_ref, col_ref, message_ref, total_ref, out_ref):
    count = row_ref.shape[0]

    def step_fn(step, carried):
        rows = pl.ds(pl.multiple_of(step * ROW_STEP, ROW_STEP), ROW_STEP)
        factor = row_ref[rows, :]
        total = jnp.zeros((ROW_STEP, LANES), jnp.float32) if total_ref is None else total_ref[rows, :]
        for start in range(0, count, COL_STEP):
            inverse = jnp.dot(factor, col_ref[:, start : start + COL_STEP], preferred_element_type=jnp.float32)
            values = lax.rsqrt(inverse).astype(jnp.bfloat16)
            total = total + jnp.dot(
                values, message_ref[start : start + COL_STEP, :], preferred_element_type=jnp.float32
            )
        out_ref[rows, :] = total
        return carried

    lax.fori_loop(0, count // ROW_STEP, step_fn, 0)


def message_geometry(message_ref, count):
    groups = count // LANES
    return tuple(message_ref[count + k * groups : count + (k + 1) * groups, :] for k in range(3))


def home_body(message_ref, out_ref, row_ref, base_ref, col_ref):
    count = row_ref.shape[0]
    geometry = message_geometry(message_ref, count)
    row_factors(geometry, base_ref, row_ref)
    column_factors(geometry, base_ref, col_ref)
    tile_product(row_ref, col_ref, message_ref, None, out_ref)


def guest_body(has_total, row_ref, message_ref, *refs):
    total_ref = refs[0] if has_total else None
    out_ref, base_ref, col_ref = refs[has_total:]
    column_factors(message_geometry(message_ref, row_ref.shape[0]), base_ref, col_ref)
    tile_product(row_ref, col_ref, message_ref, total_ref, out_ref)


def tile_scratch(count):
    return [pltpu.VMEM((8, count), jnp.float32), pltpu.VMEM((48, count), jnp.bfloat16)]


def tile_cost(count):
    flops = 2 * count * count * 256 * 2
    return pl.CostEstimate(flops=flops, bytes_accessed=3 * count * LANES * 4, transcendentals=0)


def home_tile(message, count):
    vmem = pl.BlockSpec(memory_space=pltpu.VMEM)
    return pl.pallas_call(
        home_body,
        out_shape=[
            jax.ShapeDtypeStruct((count, LANES), jnp.float32),
            jax.ShapeDtypeStruct((count, 48), jnp.bfloat16),
        ],
        in_specs=[vmem],
        out_specs=[vmem, vmem],
        scratch_shapes=tile_scratch(count),
        cost_estimate=tile_cost(count),
        compiler_params=pltpu.CompilerParams(vmem_limit_bytes=VMEM_BYTES),
        name="home_tile",
    )(message)


def guest_tile(rows, message, total, count):
    vmem = pl.BlockSpec(memory_space=pltpu.VMEM)
    operands = (rows, message) if total is None else (rows, message, total)
    return pl.pallas_call(
        functools.partial(guest_body, total is not None),
        out_shape=jax.ShapeDtypeStruct((count, LANES), jnp.float32),
        in_specs=[vmem] * len(operands),
        out_specs=vmem,
        input_output_aliases={} if total is None else {2: 0},
        scratch_shapes=tile_scratch(count),
        cost_estimate=tile_cost(count),
        compiler_params=pltpu.CompilerParams(vmem_limit_bytes=VMEM_BYTES),
        name="guest_tile",
    )(*operands)


def half_gram_body(own_ref, pair_ref, first_ref, second_ref, out_ref):
    value = 0.5 * first_ref[...] + second_ref[...]
    high = value.astype(jnp.bfloat16)
    low = (value - high.astype(jnp.float32)).astype(jnp.bfloat16)
    both = jnp.concatenate([high, low], axis=1)
    for k, ref in enumerate((own_ref, pair_ref)):
        part = lax.dot_general(
            ref[: value.shape[0], :], both, (((0,), (0,)), ((), ())), preferred_element_type=jnp.float32
        )
        out_ref[k * LANES : (k + 1) * LANES, :] = part[:, :LANES] + part[:, LANES:]


def half_gram(own, pair, first, second):
    vmem = pl.BlockSpec(memory_space=pltpu.VMEM)
    return pl.pallas_call(
        half_gram_body,
        out_shape=jax.ShapeDtypeStruct((2 * LANES, LANES), jnp.float32),
        in_specs=[vmem] * 4,
        out_specs=vmem,
        cost_estimate=pl.CostEstimate(flops=2 * 2048 * 256 * 256, bytes_accessed=3 * 2**20, transcendentals=0),
        compiler_params=pltpu.CompilerParams(vmem_limit_bytes=VMEM_BYTES),
        name="half_gram",
    )(own, pair, first, second)


def along_blk(value, sizes, target):
    ny, nx, nz, nc = sizes

    def index(y, x, z, c):
        return ((y % ny * nx + x % nx) * nz + z % nz) * nc + c % nc

    pairs = []
    for y in range(ny):
        for x in range(nx):
            for z in range(nz):
                for c in range(nc):
                    pairs.append((index(y, x, z, c), index(*target(y, x, z, c))))
    return lax.ppermute(value, BLK, pairs)


def from_shift(value, steps):
    count = lax.axis_size(BLK)
    return lax.ppermute(value, BLK, [(source, (source - steps) % count) for source in range(count)])


def from_far(value):
    count = lax.axis_size(BLK)
    return lax.ppermute(
        value, BLK, [(b, (b - 3 if b % 2 == 0 else b + 3) % count) for b in range(count)]
    )


def core_swap(value):
    return lax.ppermute(value, "core", [(0, 1), (1, 0)])


def shards(sizes, directions, axial_pos, azimuth, panel_area):
    count = axial_pos.shape[0]
    geometry = [part.reshape(count // LANES, LANES) for part in (axial_pos, azimuth, panel_area)]
    message = jnp.concatenate([directions] + geometry, axis=0)
    other = core_swap(message)
    ahead = from_shift(message, 2)
    far = from_far(message)
    pair = lax.ppermute(directions, "rhs", [(0, 1), (1, 0)])
    behind = from_shift(message, -2)
    ahead_other = core_swap(ahead)
    behind_other = core_swap(behind)

    first, rows = home_tile(message, count)
    first = guest_tile(rows, other, first, count)
    second = guest_tile(rows, ahead, None, count)
    second = guest_tile(rows, ahead_other, second, count)
    first = guest_tile(rows, far, first, count)
    half = half_gram(directions, pair, first, second)

    third = guest_tile(rows, behind, first + second, count)
    product = guest_tile(rows, behind_other, third, count)

    core = lax.axis_index("core")
    keep = jnp.where(core == 0, half[:LANES], half[LANES:])
    give = jnp.where(core == 0, half[LANES:], half[:LANES])
    value = keep + core_swap(give)
    for stage in (
        [(0, 0, 1), (0, 0, 2), (0, 0, 3)],
        [(1, 0, 0), (2, 0, 0), (3, 0, 0)],
        [(0, 0, 4), (0, 1, 0), (0, 1, 4)],
    ):
        moved = [
            along_blk(value, sizes, lambda y, x, z, c, d=d: (y + d[0], x + d[1], z + d[2], c)) for d in stage
        ]
        value = (value + moved[0]) + (moved[1] + moved[2])
    swapped = core_swap(value)
    crossed = lax.ppermute(value, ("core", "rhs"), [(3, 0), (2, 1)])
    direct = lax.ppermute(value, ("core", "rhs"), [(2, 3), (3, 2)])
    own = jnp.where(core == 0, value, swapped)
    cross = jnp.where(core == 0, swapped, value)
    cross_pair = jnp.where(core == 0, crossed, direct)
    own = own + own.T
    cross = cross + cross_pair.T
    rhs = lax.axis_index("rhs")
    gram = jnp.concatenate([jnp.where(rhs == 0, own, cross), jnp.where(rhs == 0, cross, own)], axis=0)
    return product, gram / (count * lax.axis_size(BLK))


def solution(mesh):
    sizes = (4, 2, 8, 2)
    fine = Mesh(mesh.devices.reshape(sizes + (2,)), BLK + ("rhs",))
    in_specs = (P(BLK, "rhs"), P(BLK), P(BLK), P(BLK))
    out_specs = (P(BLK, "rhs"), P(None, "rhs"))
    return jax.shard_map(
        functools.partial(shards, sizes), mesh=fine, in_specs=in_specs, out_specs=out_specs, check_vma=False
    )
```

time: 1300 us -> 124 us (0.10)
  waiting for transfers between devices: 1140 us -> 30 us
  matrix products: 104 us -> 0 us
  Pallas kernels: 0 us -> 44.5 us
  starting transfers between devices: 27.1 us -> 42.9 us
  between operations: 14.2 us -> 0.87 us
    psum x1 -> x0, waiting for transfers between devices: 1110 us -> none  [shards(): gram = lax.psum(partial_value, 'blk') / (count * lax.axis_size('blk'))]
    dot_general x29 -> x0, matrix products: 104 us -> none  [the longest x12 52.7 us: step_fn(): lax.dot_general(values, row_dirs, (((0,), (0,)), ((), ())), preferred_ele...]
    pallas_call x0 -> x8, Pallas kernels: none -> 44.5 us  [the longest x6 37.8 us: guest_tile(): pl.pallas_call(functools.partial(guest_body, total is not None), out_shap...]
    ppermute x15 -> x20, starting transfers between devices: 27.1 us -> 42.9 us  [the longest x9 17.9 us: along_blk(): return lax.ppermute(value, BLK, pairs)]
    ppermute x15 -> x20, waiting for transfers between devices: 25 us -> 30 us  [the longest x9 17.7 us: along_blk(): return lax.ppermute(value, BLK, pairs)]
  transfers between devices with their start and end apart: 17 -> 20, of which waited for: 6 -> 6; matrix products, arithmetic and copies ran while one was open for 8% -> 1% of each run, Pallas kernels for 0% -> 35%
where the time goes in v1:
time: 124 us; the launch traced here: 123 us
  Pallas kernels  44.5 us (36%)
  starting transfers between devices  42.9 us (35%)
  waiting for transfers between devices  30 us (24%)
  local copies, waits for them, and re-layouts  2.79 us (2%)
  other arithmetic  2.4 us (2%)
    pallas_call x6, Pallas kernels, guest_tile(): pl.pallas_call(functools.partial(guest_body, total is not None), out_shap...  37.8 us
    ppermute x9, starting transfers between devices, along_blk(): return lax.ppermute(value, BLK, pairs)  17.9 us
    ppermute x9, waiting for transfers between devices, along_blk(): return lax.ppermute(value, BLK, pairs)  17.7 us
    ppermute x2, starting transfers between devices, from_shift(): lax.ppermute(value, BLK, [(source, (source - steps) % count) for source i...  11.5 us
    ppermute x2, waiting for transfers between devices, from_shift(): lax.ppermute(value, BLK, [(source, (source - steps) % count) for source i...  9.39 us
    ppermute x5, starting transfers between devices, core_swap(): return lax.ppermute(value, 'core', [(0, 1), (1, 0)])  7.96 us
    pallas_call x1, Pallas kernels, home_tile(): pl.pallas_call(home_body, out_shape=[jax.ShapeDtypeStruct((count, LANES),...  5.17 us
    ppermute x1, starting transfers between devices, shards(): direct = lax.ppermute(value, ('core', 'rhs'), [(2, 3), (3, 2)])  3.06 us
  transfers between devices with their start and end apart: 20, of which 6 were waited for; matrix products, arithmetic and copies ran while one was open for 1% of the time, Pallas kernels for 35%

profile of v1, /device:TPU:1, one launch (start us, length us, event | category | flops | bytes accessed | tf_op | source)
XLA Modules:
  0.0 123.4 jit_solution(140522064983463935)
XLA Ops:
  0.6 1.2 pad_maximum_fusion.message_ref
  1.8 11.4 %collective-permute-start.4 = (bf16[2096,128]{1,0:T(8,128)(2,1)S(1)}, bf16[2096,128]{1,0:T(8,128)(2,1)}, u32[]{:S(2)}, u32[]{:S(2)}) collective-permute-start(bf16[2096,128]{1,0:T(8,128)(2,1)S(1)} %pad_maximum_fusion.message_ref), channel_id=1, source_target_pairs={{0,252},{2,254},{4,0},{6,2},{8,4},{10,6},{12,8},{14,10},{16,12},{1... | collective-permute-start | bytes 1609736 | tf_op jit(solution)/shard_map/ppermute | solution.py:184
  14.5 5.2 %home_tile.1 = (f32[2048,128]{1,0:T(8,128)S(1)}, bf16[2048,48]{1,0:T(8,128)(2,1)S(1)}) custom-call(bf16[2096,128]{1,0:T(8,128)(2,1)S(1)} %pad_maximum_fusion.message_ref), custom_call_target="tpu_custom_call" | custom-call | flops 4294967296 | bytes 3145728 | tf_op jit(solution)/shard_map/home_tile/pallas_call | solution.py:111
  20.5 9.4 %collective-permute-done.4.message_ref = bf16[2096,128]{1,0:T(8,128)(2,1)} collective-permute-done((bf16[2096,128]{1,0:T(8,128)(2,1)S(1)}, bf16[2096,128]{1,0:T(8,128)(2,1)}, u32[]{:S(2)}, u32[]{:S(2)}) %collective-permute-start.4) | collective-permute-done | bytes 536608 | tf_op jit(solution)/shard_map/ppermute | solution.py:184
  29.9 1.5 %collective-permute-start.5 = (bf16[2096,128]{1,0:T(8,128)(2,1)}, bf16[2096,128]{1,0:T(8,128)(2,1)S(1)}, u32[]{:S(2)}, u32[]{:S(2)}) collective-permute-start(bf16[2096,128]{1,0:T(8,128)(2,1)} %collective-permute-done.4.message_ref), channel_id=1, source_target_pairs={{0,2},{2,0},{1,3},{3,1},{4,6},{6,4},{5,7},{7,5},{8,10},{10,8},{9,1... | collective-permute-start | bytes 1609736 | tf_op jit(solution)/shard_map/ppermute | solution.py:195
  32.5 6.0 %guest_tile.8.refs_0_ = f32[2048,128]{1,0:T(8,128)S(1)} custom-call(bf16[2048,48]{1,0:T(8,128)(2,1)S(1)} %copy-done.2, bf16[2096,128]{1,0:T(8,128)(2,1)} %collective-permute-done.4.message_ref), custom_call_target="tpu_custom_call" | custom-call | flops 4294967296 | bytes 3145728 | tf_op jit(solution)/shard_map/guest_tile/pallas_call | solution.py:129
  38.5 6.1 %guest_tile.6.refs_0_ = f32[2048,128]{1,0:T(8,128)S(1)} custom-call(bf16[2048,48]{1,0:T(8,128)(2,1)S(1)} %copy-done.2, bf16[2096,128]{1,0:T(8,128)(2,1)} %collective-permute-done.3.message_ref, f32[2048,128]{1,0:T(8,128)S(1)} %get-tuple-element.5.refs_0_), custom_call_target="tpu_custom_call", output_to_operand_aliasing={{}: (2, {})} | custom-call | flops 4294967296 | bytes 3145728 | tf_op jit(solution)/shard_map/guest_tile/pallas_call | solution.py:129
  44.6 6.1 %guest_tile.7.first_ref = f32[2048,128]{1,0:T(8,128)S(1)} custom-call(bf16[2048,48]{1,0:T(8,128)(2,1)S(1)} %copy-done.2, bf16[2096,128]{1,0:T(8,128)(2,1)} %collective-permute-done.2.message_ref, f32[2048,128]{1,0:T(8,128)S(1)} %guest_tile.6.refs_0_), custom_call_target="tpu_custom_call", output_to_operand_aliasing={{}: (2, {})} | custom-call | flops 4294967296 | bytes 3145728 | tf_op jit(solution)/shard_map/guest_tile/pallas_call | solution.py:129
  50.7 5.0 %guest_tile.9.second_ref = f32[2048,128]{1,0:T(8,128)S(1)} custom-call(bf16[2048,48]{1,0:T(8,128)(2,1)S(1)} %copy-done.2, bf16[2096,128]{1,0:T(8,128)(2,1)S(1)} %collective-permute-done.5.message_ref, f32[2048,128]{1,0:T(8,128)S(1)} %guest_tile.8.refs_0_), custom_call_target="tpu_custom_call", output_to_operand_aliasing={{}: (2, {})} | custom-call | flops 4294967296 | bytes 3145728 | tf_op jit(solution)/shard_map/guest_tile/pallas_call | solution.py:129
  55.7 1.5 %half_gram.1 = f32[256,128]{1,0:T(8,128)S(1)} custom-call(bf16[2048,128]{1,0:T(8,128)(2,1)S(1)} %copy-done, bf16[2048,128]{1,0:T(8,128)(2,1)} %collective-permute-done.6.pair_ref, f32[2048,128]{1,0:T(8,128)S(1)} %guest_tile.7.first_ref, f32[2048,128]{1,0:T(8,128)S(1)} %guest_tile.9.second_ref), custom_call_target="tpu_custom_call" | custom-call | flops 268435456 | bytes 3145728 | tf_op jit(solution)/shard_map/half_gram/pallas_call | solution.py:156
  59.1 3.4 %collective-permute-start.9 = (f32[128,128]{1,0:T(8,128)S(1)}, f32[128,128]{1,0:T(8,128)S(1)}, u32[]{:S(2)}, u32[]{:S(2)}) collective-permute-start(f32[128,128]{1,0:T(8,128)S(1)} %select_add_fusion), channel_id=1, source_target_pairs={{0,8},{2,10},{4,12},{6,14},{8,16},{10,18},{12,20},{14,22},{16,24},... | collective-permute-start | bytes 196616 | tf_op jit(solution)/shard_map/ppermute | solution.py:179
  62.4 7.9 %collective-permute-done.10 = f32[128,128]{1,0:T(8,128)S(1)} collective-permute-done((f32[128,128]{1,0:T(8,128)S(1)}, f32[128,128]{1,0:T(8,128)S(1)}, u32[]{:S(2)}, u32[]{:S(2)}) %collective-permute-start.10) | collective-permute-done | bytes 65568 | tf_op jit(solution)/shard_map/ppermute | solution.py:179
  70.4 4.7 %collective-permute-done.8 = f32[128,128]{1,0:T(8,128)S(1)} collective-permute-done((f32[128,128]{1,0:T(8,128)S(1)}, f32[128,128]{1,0:T(8,128)S(1)}, u32[]{:S(2)}, u32[]{:S(2)}) %collective-permute-start.8) | collective-permute-done | bytes 65568 | tf_op jit(solution)/shard_map/ppermute | solution.py:179
  75.1 5.1 %collective-permute-done.9 = f32[128,128]{1,0:T(8,128)S(1)} collective-permute-done((f32[128,128]{1,0:T(8,128)S(1)}, f32[128,128]{1,0:T(8,128)S(1)}, u32[]{:S(2)}, u32[]{:S(2)}) %collective-permute-start.9) | collective-permute-done | bytes 65568 | tf_op jit(solution)/shard_map/ppermute | solution.py:179
  81.1 2.6 %collective-permute-start.12 = (f32[128,128]{1,0:T(8,128)S(1)}, f32[128,128]{1,0:T(8,128)S(1)}, u32[]{:S(2)}, u32[]{:S(2)}) collective-permute-start(f32[128,128]{1,0:T(8,128)S(1)} %add_add_fusion.2), channel_id=1, source_target_pairs={{0,128},{2,130},{4,132},{6,134},{8,136},{10,138},{12,140},{14,142}... | collective-permute-start | bytes 196616 | tf_op jit(solution)/shard_map/ppermute | solution.py:179
  84.8 2.4 %collective-permute-start.1 = (bf16[2096,128]{1,0:T(8,128)(2,1)}, bf16[2096,128]{1,0:T(8,128)(2,1)S(1)}, u32[]{:S(2)}, u32[]{:S(2)}) collective-permute-start(bf16[2096,128]{1,0:T(8,128)(2,1)} %collective-permute-done.message_ref), channel_id=1, source_target_pairs={{0,2},{2,0},{1,3},{3,1},{4,6},{6,4},{5,7},{7,5},{8,10},{10,8},{9,1... | collective-permute-start | bytes 1609736 | tf_op jit(solution)/shard_map/ppermute | solution.py:195
  88.4 4.4 %collective-permute-start.15 = (f32[128,128]{1,0:T(8,128)S(1)}, f32[128,128]{1,0:T(8,128)S(1)}, u32[]{:S(2)}, u32[]{:S(2)}) collective-permute-start(f32[128,128]{1,0:T(8,128)S(1)} %add_add_fusion.1), channel_id=1, source_target_pairs={{0,32},{2,34},{4,36},{6,38},{8,40},{10,42},{12,44},{14,46},{16,48}... | collective-permute-start | bytes 196616 | tf_op jit(solution)/shard_map/ppermute | solution.py:179
  92.9 5.0 %collective-permute-start.16 = (f32[128,128]{1,0:T(8,128)S(1)}, f32[128,128]{1,0:T(8,128)S(1)}, u32[]{:S(2)}, u32[]{:S(2)}) collective-permute-start(f32[128,128]{1,0:T(8,128)S(1)} %add_add_fusion.1), channel_id=1, source_target_pairs={{0,48},{2,50},{4,52},{6,54},{8,56},{10,58},{12,60},{14,62},{16,32}... | collective-permute-start | bytes 196616 | tf_op jit(solution)/shard_map/ppermute | solution.py:179
  97.9 7.3 %guest_tile.10.refs_0_ = f32[2048,128]{1,0:T(8,128)} custom-call(bf16[2048,48]{1,0:T(8,128)(2,1)S(1)} %copy-done.3, bf16[2096,128]{1,0:T(8,128)(2,1)} %collective-permute-done.message_ref, f32[2048,128]{1,0:T(8,128)} %add.39.refs_0_), custom_call_target="tpu_custom_call", output_to_operand_aliasing={{}: (2, {})} | custom-call | flops 4294967296 | bytes 3145728 | tf_op jit(solution)/shard_map/guest_tile/pallas_call | solution.py:129
  105.2 3.0 %collective-permute-start.17 = (f32[128,128]{1,0:T(8,128)S(1)}, f32[128,128]{1,0:T(8,128)S(1)}, u32[]{:S(2)}, u32[]{:S(2)}) collective-permute-start(f32[128,128]{1,0:T(8,128)S(1)} %add_add_fusion), channel_id=1, source_target_pairs={{0,2},{2,0},{1,3},{3,1},{4,6},{6,4},{5,7},{7,5},{8,10},{10,8},{9,1... | collective-permute-start | bytes 196616 | tf_op jit(solution)/shard_map/ppermute | solution.py:195
  108.2 7.2 %guest_tile.11 = f32[2048,128]{1,0:T(8,128)} custom-call(bf16[2048,48]{1,0:T(8,128)(2,1)S(1)} %copy-done.3, bf16[2096,128]{1,0:T(8,128)(2,1)S(1)} %collective-permute-done.1.message_ref, f32[2048,128]{1,0:T(8,128)} %guest_tile.10.refs_0_), custom_call_target="tpu_custom_call", output_to_operand_aliasing={{}: (2, {})} | custom-call | flops 4294967296 | bytes 3145728 | tf_op jit(solution)/shard_map/guest_tile/pallas_call | solution.py:129
  115.4 2.1 %collective-permute-start.18 = (f32[128,128]{1,0:T(8,128)S(1)}, f32[128,128]{1,0:T(8,128)S(1)}, u32[]{:S(2)}, u32[]{:S(2)}) collective-permute-start(f32[128,128]{1,0:T(8,128)S(1)} %add_add_fusion), channel_id=1, source_target_pairs={{3,0},{2,1},{7,4},{6,5},{11,8},{10,9},{15,12},{14,13},{19,16},{18,... | collective-permute-start | bytes 196616 | tf_op jit(solution)/shard_map/ppermute | solution.py:234
  117.5 3.1 %collective-permute-start.19 = (f32[128,128]{1,0:T(8,128)S(1)}, f32[128,128]{1,0:T(8,128)S(1)}, u32[]{:S(2)}, u32[]{:S(2)}) collective-permute-start(f32[128,128]{1,0:T(8,128)S(1)} %add_add_fusion), channel_id=1, source_target_pairs={{2,3},{3,2},{6,7},{7,6},{10,11},{11,10},{14,15},{15,14},{18,19},{1... | collective-permute-start | bytes 196616 | tf_op jit(solution)/shard_map/ppermute | solution.py:235
  120.8 1.7 %collective-permute-done.19 = f32[128,128]{1,0:T(8,128)S(1)} collective-permute-done((f32[128,128]{1,0:T(8,128)S(1)}, f32[128,128]{1,0:T(8,128)S(1)}, u32[]{:S(2)}, u32[]{:S(2)}) %collective-permute-start.19) | collective-permute-done | bytes 65568 | tf_op jit(solution)/shard_map/ppermute | solution.py:235
  (46 shorter events, 9.2 us)
Async XLA Ops:
  0.6 13.6 %copy-start = (bf16[2048,128]{1,0:T(8,128)(2,1)S(1)}, bf16[2048,128]{1,0:T(8,128)(2,1)}, u32[]{:S(2)}) copy-start(bf16[2048,128]{1,0:T(8,128)(2,1)} %own_ref.1) | copy-start | bytes 1572868
  1.8 28.0 %collective-permute-start.4 = (bf16[2096,128]{1,0:T(8,128)(2,1)S(1)}, bf16[2096,128]{1,0:T(8,128)(2,1)}, u32[]{:S(2)}, u32[]{:S(2)}) collective-permute-start(bf16[2096,128]{1,0:T(8,128)(2,1)S(1)} %pad_maximum_fusion.message_ref), channel_id=1, source_target_pairs={{0,252},{2,254},{4,0},{6,2},{8,4},{10,6},{12,8},{14,10},{16,12},{1... | collective-permute-start | bytes 1609736 | tf_op jit(solution)/shard_map/ppermute | solution.py:184
  13.2 25.3 %collective-permute-start.3 = (bf16[2096,128]{1,0:T(8,128)(2,1)S(1)}, bf16[2096,128]{1,0:T(8,128)(2,1)}, u32[]{:S(2)}, u32[]{:S(2)}) collective-permute-start(bf16[2096,128]{1,0:T(8,128)(2,1)S(1)} %pad_maximum_fusion.message_ref), channel_id=1, source_target_pairs={{0,2},{2,0},{1,3},{3,1},{4,6},{6,4},{5,7},{7,5},{8,10},{10,8},{9,1... | collective-permute-start | bytes 1609736 | tf_op jit(solution)/shard_map/ppermute | solution.py:195
  14.2 30.4 %collective-permute-start.2 = (bf16[2096,128]{1,0:T(8,128)(2,1)S(1)}, bf16[2096,128]{1,0:T(8,128)(2,1)}, u32[]{:S(2)}, u32[]{:S(2)}) collective-permute-start(bf16[2096,128]{1,0:T(8,128)(2,1)S(1)} %pad_maximum_fusion.message_ref), channel_id=1, source_target_pairs={{0,250},{2,8},{4,254},{6,12},{8,2},{10,16},{12,6},{14,20},{16,10},... | collective-permute-start | bytes 1609736 | tf_op jit(solution)/shard_map/ppermute | solution.py:189
  14.2 41.6 %collective-permute-start.6 = (bf16[2048,128]{1,0:T(8,128)(2,1)S(1)}, bf16[2048,128]{1,0:T(8,128)(2,1)}, u32[]{:S(2)}, u32[]{:S(2)}) collective-permute-start(bf16[2048,128]{1,0:T(8,128)(2,1)S(1)} %copy-done), channel_id=1, source_target_pairs={{0,1},{1,0},{2,3},{3,2},{4,5},{5,4},{6,7},{7,6},{8,9},{9,8},{10,11... | collective-permute-start | bytes 1572872 | tf_op jit(solution)/shard_map/ppermute | solution.py:205
  19.7 0.8 copy-start.1
  29.9 20.8 %collective-permute-start.5 = (bf16[2096,128]{1,0:T(8,128)(2,1)}, bf16[2096,128]{1,0:T(8,128)(2,1)S(1)}, u32[]{:S(2)}, u32[]{:S(2)}) collective-permute-start(bf16[2096,128]{1,0:T(8,128)(2,1)} %collective-permute-done.4.message_ref), channel_id=1, source_target_pairs={{0,2},{2,0},{1,3},{3,1},{4,6},{6,4},{5,7},{7,5},{8,10},{10,8},{9,1... | collective-permute-start | bytes 1609736 | tf_op jit(solution)/shard_map/ppermute | solution.py:195
  31.4 1.0 copy-start.2
  57.3 1.3 %collective-permute-start.7 = (f32[128,128]{1,0:T(8,128)S(1)}, f32[128,128]{1,0:T(8,128)S(1)}, u32[]{:S(2)}, u32[]{:S(2)}) collective-permute-start(f32[128,128]{1,0:T(8,128)S(1)} %slice_select_fusion), channel_id=1, source_target_pairs={{0,2},{2,0},{1,3},{3,1},{4,6},{6,4},{5,7},{7,5},{8,10},{10,8},{9,1... | collective-permute-start | bytes 196616 | tf_op jit(solution)/shard_map/ppermute | solution.py:195
  57.4 27.4 %collective-permute-start = (bf16[2096,128]{1,0:T(8,128)(2,1)S(1)}, bf16[2096,128]{1,0:T(8,128)(2,1)}, u32[]{:S(2)}, u32[]{:S(2)}) collective-permute-start(bf16[2096,128]{1,0:T(8,128)(2,1)S(1)} %pad_maximum_fusion.message_ref), channel_id=1, source_target_pairs={{0,4},{2,6},{4,8},{6,10},{8,12},{10,14},{12,16},{14,18},{16,20},{1... | collective-permute-start | bytes 1609736 | tf_op jit(solution)/shard_map/ppermute | solution.py:184
  58.7 11.7 %collective-permute-start.10 = (f32[128,128]{1,0:T(8,128)S(1)}, f32[128,128]{1,0:T(8,128)S(1)}, u32[]{:S(2)}, u32[]{:S(2)}) collective-permute-start(f32[128,128]{1,0:T(8,128)S(1)} %select_add_fusion), channel_id=1, source_target_pairs={{0,12},{2,14},{4,16},{6,18},{8,20},{10,22},{12,24},{14,26},{16,28}... | collective-permute-start | bytes 196616 | tf_op jit(solution)/shard_map/ppermute | solution.py:179
  59.0 16.1 %collective-permute-start.8 = (f32[128,128]{1,0:T(8,128)S(1)}, f32[128,128]{1,0:T(8,128)S(1)}, u32[]{:S(2)}, u32[]{:S(2)}) collective-permute-start(f32[128,128]{1,0:T(8,128)S(1)} %select_add_fusion), channel_id=1, source_target_pairs={{0,4},{2,6},{4,8},{6,10},{8,12},{10,14},{12,16},{14,18},{16,20},{1... | collective-permute-start | bytes 196616 | tf_op jit(solution)/shard_map/ppermute | solution.py:179
  59.1 21.1 %collective-permute-start.9 = (f32[128,128]{1,0:T(8,128)S(1)}, f32[128,128]{1,0:T(8,128)S(1)}, u32[]{:S(2)}, u32[]{:S(2)}) collective-permute-start(f32[128,128]{1,0:T(8,128)S(1)} %select_add_fusion), channel_id=1, source_target_pairs={{0,8},{2,10},{4,12},{6,14},{8,16},{10,18},{12,20},{14,22},{16,24},... | collective-permute-start | bytes 196616 | tf_op jit(solution)/shard_map/ppermute | solution.py:179
  80.1 8.1 %collective-permute-start.11 = (f32[128,128]{1,0:T(8,128)S(1)}, f32[128,128]{1,0:T(8,128)S(1)}, u32[]{:S(2)}, u32[]{:S(2)}) collective-permute-start(f32[128,128]{1,0:T(8,128)S(1)} %add_add_fusion.2), channel_id=1, source_target_pairs={{0,64},{2,66},{4,68},{6,70},{8,72},{10,74},{12,76},{14,78},{16,80}... | collective-permute-start | bytes 196616 | tf_op jit(solution)/shard_map/ppermute | solution.py:179
  81.1 7.2 %collective-permute-start.12 = (f32[128,128]{1,0:T(8,128)S(1)}, f32[128,128]{1,0:T(8,128)S(1)}, u32[]{:S(2)}, u32[]{:S(2)}) collective-permute-start(f32[128,128]{1,0:T(8,128)S(1)} %add_add_fusion.2), channel_id=1, source_target_pairs={{0,128},{2,130},{4,132},{6,134},{8,136},{10,138},{12,140},{14,142}... | collective-permute-start | bytes 196616 | tf_op jit(solution)/shard_map/ppermute | solution.py:179
  83.7 4.6 %collective-permute-start.13 = (f32[128,128]{1,0:T(8,128)S(1)}, f32[128,128]{1,0:T(8,128)S(1)}, u32[]{:S(2)}, u32[]{:S(2)}) collective-permute-start(f32[128,128]{1,0:T(8,128)S(1)} %add_add_fusion.2), channel_id=1, source_target_pairs={{0,192},{2,194},{4,196},{6,198},{8,200},{10,202},{12,204},{14,206}... | collective-permute-start | bytes 196616 | tf_op jit(solution)/shard_map/ppermute | solution.py:179
  84.8 13.1 %copy-start.3 = (bf16[2048,48]{1,0:T(8,128)(2,1)S(1)}, bf16[2048,48]{1,0:T(8,128)(2,1)}, u32[]{:S(2)}) copy-start(bf16[2048,48]{1,0:T(8,128)(2,1)} %copy-done.1) | copy-start | bytes 589828
  84.8 23.4 %collective-permute-start.1 = (bf16[2096,128]{1,0:T(8,128)(2,1)}, bf16[2096,128]{1,0:T(8,128)(2,1)S(1)}, u32[]{:S(2)}, u32[]{:S(2)}) collective-permute-start(bf16[2096,128]{1,0:T(8,128)(2,1)} %collective-permute-done.message_ref), channel_id=1, source_target_pairs={{0,2},{2,0},{1,3},{3,1},{4,6},{6,4},{5,7},{7,5},{8,10},{10,8},{9,1... | collective-permute-start | bytes 1609736 | tf_op jit(solution)/shard_map/ppermute | solution.py:195
  88.3 16.9 %collective-permute-start.14 = (f32[128,128]{1,0:T(8,128)S(1)}, f32[128,128]{1,0:T(8,128)S(1)}, u32[]{:S(2)}, u32[]{:S(2)}) collective-permute-start(f32[128,128]{1,0:T(8,128)S(1)} %add_add_fusion.1), channel_id=1, source_target_pairs={{0,16},{2,18},{4,20},{6,22},{8,24},{10,26},{12,28},{14,30},{16,0},... | collective-permute-start | bytes 196616 | tf_op jit(solution)/shard_map/ppermute | solution.py:179
  88.4 16.8 %collective-permute-start.15 = (f32[128,128]{1,0:T(8,128)S(1)}, f32[128,128]{1,0:T(8,128)S(1)}, u32[]{:S(2)}, u32[]{:S(2)}) collective-permute-start(f32[128,128]{1,0:T(8,128)S(1)} %add_add_fusion.1), channel_id=1, source_target_pairs={{0,32},{2,34},{4,36},{6,38},{8,40},{10,42},{12,44},{14,46},{16,48}... | collective-permute-start | bytes 196616 | tf_op jit(solution)/shard_map/ppermute | solution.py:179
  92.9 12.3 %collective-permute-start.16 = (f32[128,128]{1,0:T(8,128)S(1)}, f32[128,128]{1,0:T(8,128)S(1)}, u32[]{:S(2)}, u32[]{:S(2)}) collective-permute-start(f32[128,128]{1,0:T(8,128)S(1)} %add_add_fusion.1), channel_id=1, source_target_pairs={{0,48},{2,50},{4,52},{6,54},{8,56},{10,58},{12,60},{14,62},{16,32}... | collective-permute-start | bytes 196616 | tf_op jit(solution)/shard_map/ppermute | solution.py:179
  105.2 15.3 %collective-permute-start.17 = (f32[128,128]{1,0:T(8,128)S(1)}, f32[128,128]{1,0:T(8,128)S(1)}, u32[]{:S(2)}, u32[]{:S(2)}) collective-permute-start(f32[128,128]{1,0:T(8,128)S(1)} %add_add_fusion), channel_id=1, source_target_pairs={{0,2},{2,0},{1,3},{3,1},{4,6},{6,4},{5,7},{7,5},{8,10},{10,8},{9,1... | collective-permute-start | bytes 196616 | tf_op jit(solution)/shard_map/ppermute | solution.py:195
  115.4 5.4 %collective-permute-start.18 = (f32[128,128]{1,0:T(8,128)S(1)}, f32[128,128]{1,0:T(8,128)S(1)}, u32[]{:S(2)}, u32[]{:S(2)}) collective-permute-start(f32[128,128]{1,0:T(8,128)S(1)} %add_add_fusion), channel_id=1, source_target_pairs={{3,0},{2,1},{7,4},{6,5},{11,8},{10,9},{15,12},{14,13},{19,16},{18,... | collective-permute-start | bytes 196616 | tf_op jit(solution)/shard_map/ppermute | solution.py:234
  117.5 5.0 %collective-permute-start.19 = (f32[128,128]{1,0:T(8,128)S(1)}, f32[128,128]{1,0:T(8,128)S(1)}, u32[]{:S(2)}, u32[]{:S(2)}) collective-permute-start(f32[128,128]{1,0:T(8,128)S(1)} %add_add_fusion), channel_id=1, source_target_pairs={{2,3},{3,2},{6,7},{7,6},{10,11},{11,10},{14,15},{15,14},{18,19},{1... | collective-permute-start | bytes 196616 | tf_op jit(solution)/shard_map/ppermute | solution.py:235
